TPU v7x, 128 devices: a whole 4x4x4 slice. The times are simulated.
128 devices in a mesh: dp: 8 (over y_hi, x), ctx: 16 (over z, y_lo, core).
Axes of the slice: x: 4, y: 4 (y_hi: 2, y_lo: 2; y = y_hi * 2 + y_lo), z: 4, core: 2. Of those that a mesh axis runs over, the one named last changes fastest.
Arguments:
- patches: bfloat16 [16384, 1280], P(('dp', 'ctx')), may hold values from -45 to 45
- vision_gain: float32 [1280], replicated, may hold values from 0.25 to 1.75
- vision_bias: float32 [1280], replicated, may hold values from -1.75 to 1.75
- up_weight: bfloat16 [2560, 1280], P(('dp', 'ctx')), may hold values from -0.15625 to 0.15625
- down_weight: bfloat16 [2560, 1280], P(('dp', 'ctx')), may hold values from -0.125 to 0.125
- merge_gain: float32 [1280], replicated, may hold values from 0.25 to 1.75
- merge_bias: float32 [1280], replicated, may hold values from -1.75 to 1.75
- merge_weight: bfloat16 [5120, 8192], P(None, 'dp'), may hold values from -0.078125 to 0.078125
- attn_gain: float32 [8192], replicated, may hold values from 0.25 to 1.75
- query_weight: bfloat16 [8192, 4096], P(None, 'dp'), may hold values from -0.1875 to 0.1875
- kv_weight: bfloat16 [2, 8192, 1024], P(None, None, 'dp'), may hold values from -0.0625 to 0.0625
- text_query: bfloat16 [10240, 4096], P('ctx', 'dp'), may hold values from -120 to 120, as said below
- text_kv: bfloat16 [2, 10240, 1024], P(None, 'ctx', 'dp'), may hold values from -6 to 6, as said below
- doc_ids: int32 [10240], P('ctx'), may hold values from 0 to 3, never falling along the last dimension, each value on 1 to 5120 neighbouring positions
- image_sizes: int32 [128, 4], P(('dp', 'ctx')), may hold values from 1 to 16, as said below
- image_offsets: int32 [128, 4], P(('dp', 'ctx')), may hold values from 0 to 10239, as said below
Outputs:
- context: bfloat16 [10240, 4096], P('ctx', 'dp')
Inputs may be any that keep to these rules, and one draw needn't show every extreme that they name: `image_sizes`: the 4 images of one device hold 32 merged rows together, and one of them holds exactly 16. `image_offsets`: images never intersect; each lies within the 640 positions of one index of ctx; the images of one index of ctx (over all of dp) put at most 32 rows into the positions of one index of ctx, and in every draw some index of ctx takes exactly 32 rows from every index. `text_query`: rows at image positions are not read. `text_kv`: rows at image positions are not read.
All inputs are finite; a program needn't handle non-finite values.
Results may differ from a plain program's by a relative error of at most 0.035.
Values may be sent and summed in bfloat16 or wider, within the bound.
No kernel may reach another device: no remote copies, remote signals or barrier semaphores. Data moves between devices by JAX's collectives and lax.ppermute only.
A program may use at most 128 MiB of HBM per device.

v0:
```python
import math

import jax
import jax.numpy as jnp
import numpy as np
from jax import lax
from jax.experimental import pallas as pl
from jax.experimental.pallas import tpu as pltpu
from jax.sharding import Mesh
from jax.sharding import PartitionSpec as P

HEAD_DIM = 128
MOST = 16
SEQ = 640
REACH = 8
WINDOW = SEQ * (REACH + 1)
KEY_BLOCK = 640
QUERY_BLOCK = 640
GROUP = 4
IMAGES = 512
PLACE_UNROLL = 4
CAPACITY = 32
CHUNK = 16
UNITS = 24
CTX_COUNT = 16
DP_COUNT = 8

MASKED_SCORE = -1e30
LOWEST_PEAK = -1e29
EPSILON = 1e-06
DP = ("yh", "x")
CTX = ("z", "yl", "c")


def layer_norm(rows_in, norm_gain, norm_bias):
    values = rows_in.astype(jnp.float32)
    center = values - jnp.mean(values, axis=-1, keepdims=True)
    spread = jnp.mean(center * center, axis=-1, keepdims=True)
    return (center * lax.rsqrt(spread + EPSILON) * norm_gain + norm_bias).astype(jnp.bfloat16)


def quick_gelu(values):
    return values * jax.nn.sigmoid(1.702 * values)


def starts_within(sizes):
    count = sizes.shape[-1]
    earlier = jnp.arange(count)[None, :] < jnp.arange(count)[:, None]
    return jnp.sum(jnp.where(earlier, sizes[..., None, :], 0), axis=-1, dtype=jnp.int32)


def row_positions(size_table, offset_table, row_count):
    image_starts = starts_within(size_table)
    image_ends = image_starts + size_table
    within = jnp.arange(row_count, dtype=jnp.int32)[None, :, None]
    inside = (within >= image_starts[:, None, :]) & (within < image_ends[:, None, :])
    placed = offset_table[:, None, :] - image_starts[:, None, :] + within
    return jnp.sum(jnp.where(inside, placed, 0), axis=2, dtype=jnp.int32)


def gather_by_exchange(block, axes, count):
    return lax.all_to_all(
        jnp.broadcast_to(block[None], (count,) + block.shape), axes, split_axis=0, concat_axis=0
    )


def swap(rows, axis):
    return lax.ppermute(rows, axis, [(0, 1), (1, 0)])


def turn(rows, axis, by):
    return lax.ppermute(rows, axis, [(i, (i + by) % 4) for i in range(4)])


def gather_by_ring(block):
    pair = jnp.stack([block, swap(block, "yh")])
    left, right = turn(pair, "x", 1), turn(pair, "x", -1)
    across = jnp.stack([turn(left[0], "x", 1), turn(right[1], "x", -1)])
    return jnp.concatenate([pair, left, right, across], axis=0)


def attention_kernel(
    info,
    image_src,
    image_dst,
    image_len,
    blocks_at,
    text_query_ref,
    bring_ref,
    low_ref,
    last_ref,
    text_near_ref,
    text_far_ref,
    out_ref,
    text_held,
    key_wide,
    value_wide,
    image_key,
    image_value,
    image_query,
    sems,
):
    query_offset = info[1]
    near = text_near_ref.shape[0]
    copies = []
    for shard in range(REACH + 1):
        at = blocks_at[shard]
        target = text_held.at[pl.ds(shard * SEQ, SEQ), :]

        @pl.when(at < near)
        def _(at=at, target=target, shard=shard):
            pltpu.make_async_copy(text_near_ref.at[at], target, sems.at[shard]).start()

        @pl.when(at >= near)
        def _(at=at, target=target, shard=shard):
            pltpu.make_async_copy(text_far_ref.at[at - near], target, sems.at[shard]).start()

        copies.append(pltpu.make_async_copy(text_near_ref.at[0], target, sems.at[shard]))

    def widen_image(source, unused):
        for device in range(DP_COUNT):
            base = source * (DP_COUNT * CAPACITY) + device * CAPACITY
            held = last_ref[source, device * CHUNK : (device + 1) * CHUNK, :].astype(jnp.float32)
            for part in range(2):
                rows = pl.ds(pl.multiple_of(base + part * CHUNK, CHUNK), CHUNK)
                side = part * 2 * HEAD_DIM
                image_key[rows, :] = held[:, side : side + HEAD_DIM]
                image_value[rows, :] = held[:, side + HEAD_DIM : side + 2 * HEAD_DIM]
        rows = pl.ds(pl.multiple_of(source * CAPACITY, CAPACITY), CAPACITY)
        image_query[rows, :] = last_ref[source, DP_COUNT * CHUNK :, :]
        return unused

    lax.fori_loop(0, CTX_COUNT, widen_image, 0)
    for shard in range(REACH + 1):
        copies[shard].wait()

    def widen_text(step, unused):
        rows = pl.ds(pl.multiple_of(step * 320, 320), 320)
        key_wide[rows, :] = text_held[rows, :HEAD_DIM].astype(jnp.float32)
        value_wide[rows, :] = text_held[rows, HEAD_DIM:].astype(jnp.float32)
        return unused

    lax.fori_loop(0, WINDOW // 320, widen_text, 0)
    row_in = lax.broadcasted_iota(jnp.int32, (MOST, HEAD_DIM), 0)

    def place(step, unused):
        for lane in range(PLACE_UNROLL):
            image = step * PLACE_UNROLL + lane
            target = image_dst[image]
            origin = image_src[image]
            taken = row_in < image_len[image]
            rows = pl.ds(target, MOST)
            pltpu.store(key_wide.at[rows, :], image_key[pl.ds(origin, MOST), :], mask=taken)
            pltpu.store(value_wide.at[rows, :], image_value[pl.ds(origin, MOST), :], mask=taken)
        return unused

    lax.fori_loop(0, IMAGES // PLACE_UNROLL, place, 0)

    ones = jnp.ones((CHUNK, KEY_BLOCK), jnp.bfloat16)
    across = GROUP * QUERY_BLOCK
    to_power = math.log2(math.e) / math.sqrt(HEAD_DIM)
    column_at = lax.broadcasted_iota(jnp.int32, (1, QUERY_BLOCK), 1)

    def query_step(block, unused):
        rows = pl.ds(pl.multiple_of(block * QUERY_BLOCK, QUERY_BLOCK), QUERY_BLOCK)
        first = query_offset + block * QUERY_BLOCK
        bring = bring_ref[rows, :]
        is_image = jnp.max(bring.astype(jnp.float32), axis=-1, keepdims=True) > 0.5
        placed = jnp.where(
            is_image,
            jnp.dot(bring, image_query[...], preferred_element_type=jnp.float32),
            text_query_ref[rows, :].astype(jnp.float32),
        )
        queries = jnp.concatenate(
            [placed[:, h * HEAD_DIM : (h + 1) * HEAD_DIM].T for h in range(GROUP)], axis=1
        ).astype(jnp.bfloat16)
        lows = jnp.concatenate([low_ref[:, rows]] * GROUP, axis=1)
        highs = jnp.concatenate([column_at + first] * GROUP, axis=1)
        low_first = info[2 + 2 * block]
        low_last = info[3 + 2 * block]
        begin = low_first // KEY_BLOCK
        end = (first + QUERY_BLOCK - 1) // KEY_BLOCK + 1
        clear_begin = jnp.minimum((low_last + KEY_BLOCK - 1) // KEY_BLOCK, end)
        clear_end = jnp.maximum((first + 1) // KEY_BLOCK, clear_begin)

        def key_step(at, running, masked):
            peak, gathered = running
            keys_at = pl.ds(pl.multiple_of(at * KEY_BLOCK, KEY_BLOCK), KEY_BLOCK)
            scores = jnp.dot(
                key_wide[keys_at, :].astype(jnp.bfloat16),
                queries,
                preferred_element_type=jnp.float32,
            )
            values = jnp.concatenate(
                [value_wide[keys_at, :].T.astype(jnp.bfloat16), ones], axis=0
            )
            if masked:
                place_at = at * KEY_BLOCK + lax.broadcasted_iota(jnp.int32, (KEY_BLOCK, 1), 0)
                scores = jnp.where((place_at >= lows) & (place_at <= highs), scores, MASKED_SCORE)
            new_peak = jnp.maximum(peak, jnp.max(scores, axis=0, keepdims=True))
            weights = jnp.exp2((scores - new_peak) * to_power).astype(jnp.bfloat16)
            rescale = jnp.exp2((peak - new_peak) * to_power)
            gathered = gathered * rescale + jnp.dot(
                values, weights, preferred_element_type=jnp.float32
            )
            return new_peak, gathered

        running = (
            jnp.full((1, across), LOWEST_PEAK, jnp.float32),
            jnp.zeros((HEAD_DIM + CHUNK, across), jnp.float32),
        )
        running = lax.fori_loop(begin, clear_begin, lambda a, r: key_step(a, r, True), running)
        running = lax.fori_loop(clear_begin, clear_end, lambda a, r: key_step(a, r, False), running)
        peak, gathered = lax.fori_loop(clear_end, end, lambda a, r: key_step(a, r, True), running)
        context = gathered[:HEAD_DIM] / gathered[HEAD_DIM : HEAD_DIM + 1]
        for h in range(GROUP):
            out_ref[rows, h * HEAD_DIM : (h + 1) * HEAD_DIM] = context[
                :, h * QUERY_BLOCK : (h + 1) * QUERY_BLOCK
            ].T.astype(jnp.bfloat16)
        return unused

    lax.fori_loop(0, SEQ // QUERY_BLOCK, query_step, 0)


def attention(tables, text_query, bring_in, low_rows, last, text):
    smem = pl.BlockSpec(memory_space=pltpu.SMEM)
    vmem = pl.BlockSpec(memory_space=pltpu.VMEM)
    image_rows = CTX_COUNT * DP_COUNT * CAPACITY
    return pl.pallas_call(
        attention_kernel,
        out_shape=jax.ShapeDtypeStruct(text_query.shape, jnp.bfloat16),
        in_specs=[smem] * 5 + [vmem] * 4 + [pl.BlockSpec(memory_space=pl.ANY)] * 2,
        out_specs=vmem,
        scratch_shapes=[
            pltpu.VMEM((WINDOW, 2 * HEAD_DIM), jnp.bfloat16),
            pltpu.VMEM((WINDOW + MOST, HEAD_DIM), jnp.float32),
            pltpu.VMEM((WINDOW + MOST, HEAD_DIM), jnp.float32),
            pltpu.VMEM((image_rows + MOST, HEAD_DIM), jnp.float32),
            pltpu.VMEM((image_rows + MOST, HEAD_DIM), jnp.float32),
            pltpu.VMEM((CTX_COUNT * CAPACITY, GROUP * HEAD_DIM), jnp.bfloat16),
            pltpu.SemaphoreType.DMA((REACH + 1,)),
        ],
        compiler_params=pltpu.CompilerParams(vmem_limit_bytes=48 * 1024 * 1024),
        cost_estimate=pl.CostEstimate(
            flops=8_000_000_000, bytes_accessed=8_000_000, transcendentals=13_000_000
        ),
    )(*tables, text_query, bring_in, low_rows, last, *text)


def project_kernel(
    order_ref,
    first_ref,
    second_ref,
    gain_ref,
    query_weight_ref,
    kv_weight_ref,
    query_ref,
    kv_ref,
    query_sum,
    kv_sum,
    squares,
):
    step = pl.program_id(0)

    @pl.when(step == 0)
    def _():
        query_sum[...] = jnp.zeros_like(query_sum)
        kv_sum[...] = jnp.zeros_like(kv_sum)
        squares[...] = jnp.zeros_like(squares)

    values = jnp.concatenate([first_ref[0], second_ref[0]], axis=0).astype(jnp.float32)
    squares[...] += jnp.sum(values * values, axis=-1, keepdims=True)
    gained = (values * gain_ref[0]).astype(jnp.bfloat16)
    query_sum[...] += jnp.dot(gained, query_weight_ref[...], preferred_element_type=jnp.float32)
    kv_sum[:, :HEAD_DIM] += jnp.dot(gained, kv_weight_ref[0], preferred_element_type=jnp.float32)
    kv_sum[:, HEAD_DIM:] += jnp.dot(gained, kv_weight_ref[1], preferred_element_type=jnp.float32)

    @pl.when(step == DP_COUNT - 1)
    def _():
        scale = lax.rsqrt(squares[...] / (DP_COUNT * first_ref.shape[2]) + EPSILON)
        query_ref[...] = (query_sum[...] * scale).astype(jnp.bfloat16)
        kv = (kv_sum[...] * scale).astype(jnp.bfloat16)
        half = first_ref.shape[1]
        kv_ref[:, : 2 * HEAD_DIM] = kv[:half]
        kv_ref[:, 2 * HEAD_DIM :] = kv[half:]


def project(order, wholes, gain, query_weight, kv_weight):
    count, rows, part = wholes[0].shape
    query_width, kv_width = query_weight.shape[1], kv_weight.shape[2]
    rows_spec = pl.BlockSpec((1, rows, part), lambda k, order: (k, 0, 0))
    return pl.pallas_call(
        project_kernel,
        grid_spec=pltpu.PrefetchScalarGridSpec(
            num_scalar_prefetch=1,
            grid=(count,),
            in_specs=[
                rows_spec,
                rows_spec,
                pl.BlockSpec((1, 1, part), lambda k, order: (order[k], 0, 0)),
                pl.BlockSpec((part, query_width), lambda k, order: (order[k], 0)),
                pl.BlockSpec((2, part, kv_width), lambda k, order: (0, order[k], 0)),
            ],
            out_specs=(
                pl.BlockSpec((2 * rows, query_width), lambda k, order: (0, 0)),
                pl.BlockSpec((rows, 4 * kv_width), lambda k, order: (0, 0)),
            ),
            scratch_shapes=[
                pltpu.VMEM((2 * rows, query_width), jnp.float32),
                pltpu.VMEM((2 * rows, 2 * kv_width), jnp.float32),
                pltpu.VMEM((2 * rows, 1), jnp.float32),
            ],
        ),
        out_shape=(
            jax.ShapeDtypeStruct((2 * rows, query_width), jnp.bfloat16),
            jax.ShapeDtypeStruct((rows, 4 * kv_width), jnp.bfloat16),
        ),
        compiler_params=pltpu.CompilerParams(vmem_limit_bytes=20 * 1024 * 1024),
        cost_estimate=pl.CostEstimate(
            flops=4 * rows * count * part * (query_width + 2 * kv_width),
            bytes_accessed=2 * count * part * (query_width + 2 * kv_width + 2 * rows),
            transcendentals=0,
        ),
    )(order, *wholes, gain, query_weight, kv_weight)


def body(
    patches,
    vision_gain,
    vision_bias,
    up_weight,
    down_weight,
    merge_gain,
    merge_bias,
    merge_weight,
    attn_gain,
    query_weight,
    kv_weight,
    text_query,
    text_kv,
    doc_ids,
    image_sizes,
    image_offsets,
):
    z_at, yl_at, c_at = lax.axis_index("z"), lax.axis_index("yl"), lax.axis_index("c")
    ctx_index = lax.axis_index(CTX)
    width = patches.shape[1]
    own_rows = patches.shape[0]
    units_own = up_weight.shape[0]

    below = jnp.sum(
        (doc_ids[:, None] < jnp.arange(4, dtype=jnp.int32)[None, :]).astype(jnp.int32),
        axis=0,
        dtype=jnp.int32,
    )
    facts = jnp.concatenate([image_sizes, image_offsets, below[None, :]], axis=1)
    facts = jnp.concatenate([facts // 128, facts % 128], axis=1).astype(jnp.bfloat16)
    fact_count = facts.shape[1]
    block = jnp.concatenate(
        [
            jnp.pad(up_weight, ((0, UNITS - units_own), (0, 0))),
            down_weight,
            jnp.pad(facts, ((0, UNITS - units_own - 1), (0, width - fact_count))),
        ],
        axis=0,
    )
    block = jnp.broadcast_to(block[None], (16,) + block.shape)
    block, patches = lax.optimization_barrier((block, patches))
    units = lax.all_to_all(block, DP + ("yl",), split_axis=0, concat_axis=0)
    text = jnp.concatenate([text_kv[0], text_kv[1]], axis=1)
    text, units = lax.optimization_barrier((text, units))
    text_beside = swap(text, "yl")
    normed = layer_norm(patches, vision_gain, vision_bias)
    column = jnp.concatenate(
        [normed]
        + [
            lax.ppermute(normed, "z", [(i, (i + step) % 4) for i in range(4)])
            for step in (1, 2, 3)
        ],
        axis=0,
    )
    near_rows = column.shape[0]
    near = jnp.concatenate([column, swap(column, "c")], axis=0)
    ups = units[:, :UNITS].reshape(-1, width)
    downs = units[:, UNITS:].reshape(-1, width)
    facts = units[:, UNITS + units_own, :fact_count].reshape(1, -1)
    hidden = quick_gelu(
        lax.dot_general(near, ups, (((1,), (1,)), ((), ())), preferred_element_type=jnp.float32)
    ).astype(jnp.bfloat16)
    away = jnp.dot(hidden[near_rows:], downs, preferred_element_type=jnp.float32).astype(
        jnp.bfloat16
    )
    here = jnp.dot(hidden[:near_rows], downs, preferred_element_type=jnp.float32)
    came = swap(
        jnp.concatenate(
            [away, jnp.pad(facts, ((0, CHUNK - 1), (0, width - facts.shape[1])))], axis=0
        ),
        "c",
    )
    text_beside, came = lax.optimization_barrier((text_beside, came))
    text = jnp.concatenate([text, text_beside], axis=0)
    pair_sum = (here + came[:near_rows].astype(jnp.float32)).astype(jnp.bfloat16)
    other = came[near_rows : near_rows + 1, : facts.shape[1]]
    facts = jnp.concatenate(
        [jnp.where(c_at == 0, facts, other), jnp.where(c_at == 0, other, facts)], axis=1
    )
    tail = jnp.pad(facts, ((0, CHUNK - 1), (0, width - facts.shape[1])))
    by_z = pair_sum.reshape(4, own_rows, width)
    terms = lax.all_to_all(
        jnp.stack(
            [
                jnp.concatenate(
                    [lax.dynamic_index_in_dim(by_z, (z_at - j + 4) % 4, 0, False), tail], axis=0
                )
                for j in range(4)
            ]
        ),
        "z",
        split_axis=0,
        concat_axis=0,
    )
    branch = jnp.sum(terms[:, :own_rows].astype(jnp.float32), axis=0)
    facts = terms[:, own_rows, : facts.shape[1]].astype(jnp.int32)
    facts = facts.reshape(4, 2, 8, 2, fact_count).transpose(2, 0, 3, 1, 4)
    facts = facts.reshape(8, 16, 2, fact_count // 2)
    facts = facts[:, :, 0] * 128 + facts[:, :, 1]
    vision = (patches.astype(jnp.float32) + branch).astype(jnp.bfloat16)
    merged_in = layer_norm(vision, merge_gain, merge_bias).reshape(-1, 4 * width)

    text, merged_in = lax.optimization_barrier((text, merged_in))
    text = jnp.concatenate(
        [
            text,
            lax.ppermute(text, "z", [(0, 1), (1, 2), (2, 3)]),
            lax.ppermute(text, "z", [(0, 2), (1, 3)]),
        ],
        axis=0,
    )
    yh_at, x_at = lax.axis_index("yh"), lax.axis_index("x")
    step = jnp.array([0, 0, 3, 3, 1, 1, 2, 2], jnp.int32)
    order = (yh_at ^ (jnp.arange(8, dtype=jnp.int32) % 2)) * 4 + (x_at + step) % 4
    member = jnp.arange(8, dtype=jnp.int32)
    slot_of = jnp.sum(
        jnp.where(member[:, None] == order[None, :], member[None, :], 0), axis=1, dtype=jnp.int32
    )
    columns = [
        gather_by_ring(merged_in[at : at + CHUNK]).reshape(-1, 4 * width) for at in (0, CHUNK)
    ]
    spread_rows = []
    for column_in in columns:
        merged = jnp.dot(column_in, merge_weight, preferred_element_type=jnp.float32).astype(
            jnp.bfloat16
        )
        by_member = merged.reshape(DP_COUNT, CHUNK, -1)
        spread_rows.append(
            jnp.concatenate(
                [lax.dynamic_index_in_dim(by_member, slot_of[d], 0, False) for d in range(8)],
                axis=0,
            )
        )
    text, spread_rows[1] = lax.optimization_barrier((text, spread_rows[1]))
    wholes = [gather_by_ring(rows) for rows in spread_rows]
    gains = attn_gain.reshape(DP_COUNT, 1, -1)
    image_query, image_kv = project(order, wholes, gains, query_weight, kv_weight)
    text = [half.reshape(6, SEQ, -1) for half in (text, swap(text, "c"))]

    sizes = jnp.swapaxes(facts[:, :, :4], 0, 1)
    offsets = jnp.swapaxes(facts[:, :, 4:8], 0, 1)
    starts = jnp.sum(facts[0, :, 8:], axis=0, dtype=jnp.int32)
    positions = row_positions(sizes.reshape(128, 4), offsets.reshape(128, 4), CAPACITY).reshape(
        16, 256
    )
    before = jnp.arange(256)[None, :] < jnp.arange(256)[:, None]
    own_owner = lax.dynamic_index_in_dim(positions, ctx_index, 0, False) // SEQ
    own_rank = jnp.sum(
        ((own_owner[None, :] == own_owner[:, None]) & before).astype(jnp.int32),
        axis=1,
        dtype=jnp.int32,
    )
    own_slot = (own_owner * CAPACITY + own_rank).reshape(8, 2, CHUNK).swapaxes(0, 1).reshape(-1)
    spread_out = (jnp.arange(512, dtype=jnp.int32)[:, None] == own_slot[None, :]).astype(
        jnp.bfloat16
    )
    mine = positions // SEQ == ctx_index
    rank = jnp.sum((mine[:, None, :] & before[None]).astype(jnp.int32), axis=2, dtype=jnp.int32)
    slot_here = mine[:, :, None] & (
        rank[:, :, None] == jnp.arange(CAPACITY, dtype=jnp.int32)[None, None, :]
    )
    slot_place = jnp.sum(
        jnp.where(slot_here, positions[:, :, None] - ctx_index * SEQ + 1, 0),
        axis=1,
        dtype=jnp.int32,
    ).reshape(-1) - 1
    bring_in = jnp.arange(SEQ, dtype=jnp.int32)[:, None] == slot_place[None, :]

    sent = jnp.dot(spread_out, image_query, preferred_element_type=jnp.float32).astype(jnp.bfloat16)
    last = lax.all_to_all(
        jnp.concatenate(
            [
                jnp.broadcast_to(image_kv[None], (CTX_COUNT,) + image_kv.shape),
                sent.reshape(CTX_COUNT, CAPACITY, -1),
            ],
            axis=1,
        ),
        CTX,
        split_axis=0,
        concat_axis=0,
    )

    window_start = jnp.maximum(ctx_index - REACH, 0) * SEQ
    low_rows = (
        jnp.sum(
            jnp.where(
                doc_ids[:, None] == jnp.arange(4, dtype=jnp.int32)[None, :], starts[None, :], 0
            ),
            axis=1,
            dtype=jnp.int32,
        )
        - window_start
    )
    low_rows = jnp.maximum(low_rows, 0)
    edges = low_rows.reshape(-1, QUERY_BLOCK)
    info = jnp.concatenate(
        [
            jnp.stack([window_start, ctx_index * SEQ - window_start]).astype(jnp.int32),
            jnp.stack([edges[:, 0], edges[:, -1]], axis=1).reshape(-1),
        ]
    )
    within_device = starts_within(sizes)
    shard = window_start // SEQ + jnp.arange(REACH + 1, dtype=jnp.int32)
    text_at = (
        ((shard % 2) ^ c_at) * 6
        + jnp.clip(z_at - shard // 4, 0, 2) * 2
        + ((shard // 2 % 2) ^ yl_at)
    )
    image_src = (
        jnp.arange(CTX_COUNT * DP_COUNT, dtype=jnp.int32).reshape(CTX_COUNT, DP_COUNT, 1) * CAPACITY
        + within_device
    )
    targets = (offsets - window_start).reshape(-1)
    inside = (targets >= 0) & (targets < WINDOW)
    tables = (
        info,
        image_src.reshape(-1),
        jnp.where(inside, targets, 0),
        jnp.where(inside, sizes.reshape(-1), 0),
        text_at.astype(jnp.int32),
    )
    return attention(
        tables, text_query, bring_in.astype(jnp.bfloat16), low_rows[None, :], last, text
    )


def solution(mesh):
    fine = Mesh(mesh.devices.reshape(2, 4, 4, 2, 2), DP + CTX)
    every = DP + CTX
    return jax.shard_map(
        body,
        mesh=fine,
        in_specs=(
            P(every, None),
            P(),
            P(),
            P(every, None),
            P(every, None),
            P(),
            P(),
            P(None, DP),
            P(),
            P(None, DP),
            P(None, None, DP),
            P(CTX, DP),
            P(None, CTX, DP),
            P(CTX),
            P(every, None),
            P(every, None),
        ),
        out_specs=P(CTX, DP),
        check_vma=False,
    )
```

profile of v0, /device:TPU:79, one launch (start us, length us, event | category | flops | bytes accessed | tf_op | source)
XLA Modules:
  0.0 264.9 jit_solution(12021813438036293261)
XLA Ops:
  7.9 6.7 %all-to-all-start = ((bf16[16,48,1280]{2,1,0:T(8,128)(2,1)}), bf16[16,48,1280]{2,1,0:T(8,128)(2,1)S(1)}, u32[]{:S(2)}, u32[]{:S(2)}) async-start(bf16[16,48,1280]{2,1,0:T(8,128)(2,1)} %broadcast_in_dim.71), calls=%async_computation | async-start | bytes 3932160 | tf_op jit(solution)/shard_map/all_to_all | solution.py:369
  14.7 5.9 %collective-permute-done.1 = bf16[128,1280]{1,0:T(8,128)(2,1)S(1)} collective-permute-done((bf16[128,1280]{1,0:T(8,128)(2,1)S(1)}, bf16[128,1280]{1,0:T(8,128)(2,1)S(1)}, u32[]{:S(2)}, u32[]{:S(2)}) %collective-permute-start.1) | collective-permute-done | bytes 327712 | tf_op jit(solution)/shard_map/ppermute | solution.py:377
  30.8 8.8 %all-to-all-done = bf16[16,48,1280]{2,1,0:T(8,128)(2,1)S(1)} async-done(((bf16[16,48,1280]{2,1,0:T(8,128)(2,1)}), bf16[16,48,1280]{2,1,0:T(8,128)(2,1)S(1)}, u32[]{:S(2)}, u32[]{:S(2)}) %all-to-all-start) | async-done | bytes 1966112 | tf_op jit(solution)/shard_map/all_to_all | solution.py:369
  40.8 3.7 %multiply_convert_fusion = bf16[1024,384]{1,0:T(8,128)(2,1)S(1)} fusion(bf16[1024,1280]{1,0:T(8,128)(2,1)} %constant_dynamic-update-slice_fusion, bf16[384,1280]{1,0:T(8,128)(2,1)} %bitcast.195), kind=kOutput, calls=%fused_computation.8 | convolution fusion | flops 1008992256 | bytes 4390912 | tf_op jit(solution)/shard_map/dot_general | solution.py:388
  48.5 7.1 %collective-permute-done.4 = bf16[640,256]{1,0:T(8,128)(2,1)} collective-permute-done((bf16[640,256]{1,0:T(8,128)(2,1)S(1)}, bf16[640,256]{1,0:T(8,128)(2,1)}, u32[]{:S(2)}, u32[]{:S(2)}) %collective-permute-start.4) | collective-permute-done | bytes 327712 | tf_op jit(solution)/shard_map/ppermute | solution.py:68
  60.2 6.2 %all-to-all-start.1 = ((bf16[4,144,1280]{2,1,0:T(8,128)(2,1)}), bf16[4,144,1280]{2,1,0:T(8,128)(2,1)S(1)}, u32[]{:S(2)}, u32[]{:S(2)}) async-start(bf16[4,144,1280]{2,1,0:T(8,128)(2,1)} %pad_maximum_fusion.2), calls=%async_computation.1 | async-start | bytes 2949120 | tf_op jit(solution)/shard_map/all_to_all | solution.py:409
  90.0 2.8 %collective-permute-start.16 = (bf16[1280,256]{1,0:T(8,128)(2,1)}, bf16[1280,256]{1,0:T(8,128)(2,1)}, u32[]{:S(2)}, u32[]{:S(2)}) collective-permute-start(bf16[1280,256]{1,0:T(8,128)(2,1)} %pad_maximum_fusion.8), channel_id=1, source_target_pairs={{0,4},{4,8},{8,12},{1,5},{5,9},{9,13},{2,6},{6,10},{10,14},{3,7},{... | collective-permute-start | bytes 1966088 | tf_op jit(solution)/shard_map/ppermute | solution.py:434
  99.7 3.1 %collective-permute-start.7 = (bf16[2,16,5120]{2,1,0:T(8,128)(2,1)S(1)}, bf16[2,16,5120]{2,1,0:T(8,128)(2,1)S(1)}, u32[]{:S(2)}, u32[]{:S(2)}) collective-permute-start(bf16[2,16,5120]{2,1,0:T(8,128)(2,1)S(1)} %pad_maximum_fusion.12), channel_id=1, source_target_pairs={{0,16},{16,32},{32,48},{48,0},{1,17},{17,33},{33,49},{49,1},{2,18}... | collective-permute-start | bytes 983048 | tf_op jit(solution)/shard_map/ppermute | solution.py:72
  111.0 3.7 %collective-permute-done.19 = bf16[2,16,5120]{2,1,0:T(8,128)(2,1)S(1)} collective-permute-done((bf16[2,16,5120]{2,1,0:T(8,128)(2,1)S(1)}, bf16[2,16,5120]{2,1,0:T(8,128)(2,1)S(1)}, u32[]{:S(2)}, u32[]{:S(2)}) %collective-permute-start.19) | collective-permute-done | bytes 327712 | tf_op jit(solution)/shard_map/ppermute | solution.py:72
  114.8 3.2 %collective-permute-done.20 = bf16[2,16,5120]{2,1,0:T(8,128)(2,1)S(1)} collective-permute-done((bf16[2,16,5120]{2,1,0:T(8,128)(2,1)S(1)}, bf16[2,16,5120]{2,1,0:T(8,128)(2,1)S(1)}, u32[]{:S(2)}, u32[]{:S(2)}) %collective-permute-start.20) | collective-permute-done | bytes 327712 | tf_op jit(solution)/shard_map/ppermute | solution.py:72
  119.6 3.5 %collective-permute-done.16 = bf16[1280,256]{1,0:T(8,128)(2,1)} collective-permute-done((bf16[1280,256]{1,0:T(8,128)(2,1)}, bf16[1280,256]{1,0:T(8,128)(2,1)}, u32[]{:S(2)}, u32[]{:S(2)}) %collective-permute-start.16) | collective-permute-done | bytes 655392 | tf_op jit(solution)/shard_map/ppermute | solution.py:434
  126.2 6.0 %convolution_convert_fusion.3 = bf16[128,1024]{1,0:T(8,128)(2,1)S(1)} fusion(bf16[128,5120]{1,0:T(8,128)(2,1)} %bitcast.169, bf16[5120,1024]{1,0:T(8,128)(2,1)} %param.24), kind=kOutput, calls=%fused_computation.16 | convolution fusion | flops 1342308352 | bytes 12058624 | tf_op jit(solution)/shard_map/dot_general | solution.py:451
  137.4 3.6 %collective-permute-done.11 = bf16[128,1024]{1,0:T(8,128)(2,1)S(1)} collective-permute-done((bf16[128,1024]{1,0:T(8,128)(2,1)S(1)}, bf16[128,1024]{1,0:T(8,128)(2,1)S(1)}, u32[]{:S(2)}, u32[]{:S(2)}) %collective-permute-start.11) | collective-permute-done | bytes 262176 | tf_op jit(solution)/shard_map/ppermute | solution.py:68
  141.0 3.1 %collective-permute-start.12 = (bf16[2,128,1024]{2,1,0:T(8,128)(2,1)S(1)}, bf16[2,128,1024]{2,1,0:T(8,128)(2,1)S(1)}, u32[]{:S(2)}, u32[]{:S(2)}) collective-permute-start(bf16[2,128,1024]{2,1,0:T(8,128)(2,1)S(1)} %pad_maximum_fusion.9), channel_id=1, source_target_pairs={{0,16},{16,32},{32,48},{48,0},{1,17},{17,33},{33,49},{49,1},{2,18}... | collective-permute-start | bytes 1572872 | tf_op jit(solution)/shard_map/ppermute | solution.py:72
  147.0 3.3 %collective-permute-done.12 = bf16[2,128,1024]{2,1,0:T(8,128)(2,1)S(1)} collective-permute-done((bf16[2,128,1024]{2,1,0:T(8,128)(2,1)S(1)}, bf16[2,128,1024]{2,1,0:T(8,128)(2,1)S(1)}, u32[]{:S(2)}, u32[]{:S(2)}) %collective-permute-start.12) | collective-permute-done | bytes 524320 | tf_op jit(solution)/shard_map/ppermute | solution.py:72
  150.2 3.2 %collective-permute-start.14 = (bf16[128,1024]{1,0:T(8,128)(2,1)S(1)}, bf16[128,1024]{1,0:T(8,128)(2,1)S(1)}, u32[]{:S(2)}, u32[]{:S(2)}) collective-permute-start(bf16[128,1024]{1,0:T(8,128)(2,1)S(1)} %slice_bitcast_fusion.3), channel_id=1, source_target_pairs={{0,16},{16,32},{32,48},{48,0},{1,17},{17,33},{33,49},{49,1},{2,18}... | collective-permute-start | bytes 786440 | tf_op jit(solution)/shard_map/ppermute | solution.py:72
  153.5 6.2 %collective-permute-done.24 = bf16[2,128,1024]{2,1,0:T(8,128)(2,1)S(1)} collective-permute-done((bf16[2,128,1024]{2,1,0:T(8,128)(2,1)S(1)}, bf16[2,128,1024]{2,1,0:T(8,128)(2,1)S(1)}, u32[]{:S(2)}, u32[]{:S(2)}) %collective-permute-start.24) | collective-permute-done | bytes 524320 | tf_op jit(solution)/shard_map/ppermute | solution.py:72
  159.8 3.5 %collective-permute-start.26 = (bf16[128,1024]{1,0:T(8,128)(2,1)S(1)}, bf16[128,1024]{1,0:T(8,128)(2,1)S(1)}, u32[]{:S(2)}, u32[]{:S(2)}) collective-permute-start(bf16[128,1024]{1,0:T(8,128)(2,1)S(1)} %slice_bitcast_fusion.1), channel_id=1, source_target_pairs={{0,16},{16,32},{32,48},{48,0},{1,17},{17,33},{33,49},{49,1},{2,18}... | collective-permute-start | bytes 786440 | tf_op jit(solution)/shard_map/ppermute | solution.py:72
  165.4 3.1 %collective-permute-done.15 = bf16[128,1024]{1,0:T(8,128)(2,1)S(1)} collective-permute-done((bf16[128,1024]{1,0:T(8,128)(2,1)S(1)}, bf16[128,1024]{1,0:T(8,128)(2,1)S(1)}, u32[]{:S(2)}, u32[]{:S(2)}) %collective-permute-start.15) | collective-permute-done | bytes 262176 | tf_op jit(solution)/shard_map/ppermute | solution.py:72
  171.0 3.1 %collective-permute-done.27 = bf16[128,1024]{1,0:T(8,128)(2,1)S(1)} collective-permute-done((bf16[128,1024]{1,0:T(8,128)(2,1)S(1)}, bf16[128,1024]{1,0:T(8,128)(2,1)S(1)}, u32[]{:S(2)}, u32[]{:S(2)}) %collective-permute-start.27) | collective-permute-done | bytes 262176 | tf_op jit(solution)/shard_map/ppermute | solution.py:72
  174.2 6.9 %shard_map.163 = (bf16[256,512]{1,0:T(8,128)(2,1)S(1)}, bf16[128,512]{1,0:T(8,128)(2,1)S(1)}) custom-call(s32[8]{0:T(128)S(1)} %fusion.49.order_ref, bf16[8,128,1024]{2,1,0:T(8,128)(2,1)S(1)} %bitcast_dynamic-update-slice_fusion.2.first_ref, bf16[8,128,1024]{2,1,0:T(8,128)(2,1)S(1)} %bitcast_dynamic-update-slice_fusion.second_ref, ...), custom_call_target="tpu_custom_call" | custom-call | flops 3221225472 | bytes 16777216 | tf_op jit(solution)/shard_map/pallas_call | solution.py:292
  183.4 16.8 %all-to-all-start.2 = ((bf16[16,160,512]{2,1,0:T(8,128)(2,1)}), bf16[16,160,512]{2,1,0:T(8,128)(2,1)}, u32[]{:S(2)}, u32[]{:S(2)}) async-start(bf16[16,160,512]{2,1,0:T(8,128)(2,1)} %pad_maximum_fusion), calls=%async_computation.2 | async-start | bytes 5242880 | tf_op jit(solution)/shard_map/all_to_all | solution.py:497
  204.8 26.1 %all-to-all-done.2.last_ref = bf16[16,160,512]{2,1,0:T(8,128)(2,1)} async-done(((bf16[16,160,512]{2,1,0:T(8,128)(2,1)}), bf16[16,160,512]{2,1,0:T(8,128)(2,1)}, u32[]{:S(2)}, u32[]{:S(2)}) %all-to-all-start.2) | async-done | bytes 2621472 | tf_op jit(solution)/shard_map/all_to_all | solution.py:497
  230.9 33.8 %shard_map.164 = bf16[640,512]{1,0:T(8,128)(2,1)} custom-call(s32[4]{0:T(128)S(1)} %pad_add_fusion.1.info, s32[512]{0:T(512)S(1)} %add.310.image_src, s32[512]{0:T(512)S(1)} %get-tuple-element.67.image_dst, s32[512]{0:T(512)S(1)} %get-tuple-element.66.image_len, s32[9]{0:T(128)S(1)} %fusion.56.blocks_at, bf16[640,512]{1,0:T(8,128)(2,1)S(1)} %copy-done.2, ...), custom_call_target="tpu_custom_call" | custom-call | flops 8000000000 | bytes 8000000 | tf_op jit(solution)/shard_map/pallas_call | solution.py:229
  (246 shorter events, 75.2 us)
Async XLA Ops:
  5.4 9.3 %collective-permute-start = (bf16[128,1280]{1,0:T(8,128)(2,1)S(1)}, bf16[128,1280]{1,0:T(8,128)(2,1)S(1)}, u32[]{:S(2)}, u32[]{:S(2)}) collective-permute-start(bf16[128,1280]{1,0:T(8,128)(2,1)S(1)} %get-tuple-element.36), channel_id=1, source_target_pairs={{0,4},{4,8},{8,12},{12,0},{1,5},{5,9},{9,13},{13,1},{2,6},{6,10},{... | collective-permute-start | bytes 983048 | tf_op jit(solution)/shard_map/ppermute | solution.py:377
  6.7 13.8 %collective-permute-start.1 = (bf16[128,1280]{1,0:T(8,128)(2,1)S(1)}, bf16[128,1280]{1,0:T(8,128)(2,1)S(1)}, u32[]{:S(2)}, u32[]{:S(2)}) collective-permute-start(bf16[128,1280]{1,0:T(8,128)(2,1)S(1)} %get-tuple-element.36), channel_id=1, source_target_pairs={{0,8},{4,12},{8,0},{12,4},{1,9},{5,13},{9,1},{13,5},{2,10},{6,14},... | collective-permute-start | bytes 983048 | tf_op jit(solution)/shard_map/ppermute | solution.py:377
  6.7 15.9 %collective-permute-start.2 = (bf16[128,1280]{1,0:T(8,128)(2,1)S(1)}, bf16[128,1280]{1,0:T(8,128)(2,1)}, u32[]{:S(2)}, u32[]{:S(2)}) collective-permute-start(bf16[128,1280]{1,0:T(8,128)(2,1)S(1)} %get-tuple-element.36), channel_id=1, source_target_pairs={{0,12},{4,0},{8,4},{12,8},{1,13},{5,1},{9,5},{13,9},{2,14},{6,2},{... | collective-permute-start | bytes 983048 | tf_op jit(solution)/shard_map/ppermute | solution.py:377
  7.9 31.7 %all-to-all-start = ((bf16[16,48,1280]{2,1,0:T(8,128)(2,1)}), bf16[16,48,1280]{2,1,0:T(8,128)(2,1)S(1)}, u32[]{:S(2)}, u32[]{:S(2)}) async-start(bf16[16,48,1280]{2,1,0:T(8,128)(2,1)} %broadcast_in_dim.71), calls=%async_computation | async-start | bytes 3932160 | tf_op jit(solution)/shard_map/all_to_all | solution.py:369
  45.5 10.2 %collective-permute-start.5 = (bf16[528,1280]{1,0:T(8,128)(2,1)S(1)}, bf16[528,1280]{1,0:T(8,128)(2,1)}, u32[]{:S(2)}, u32[]{:S(2)}) collective-permute-start(bf16[528,1280]{1,0:T(8,128)(2,1)S(1)} %fusion.1), channel_id=1, source_target_pairs={{0,1},{1,0},{2,3},{3,2},{4,5},{5,4},{6,7},{7,6},{8,9},{9,8},{10,11... | collective-permute-start | bytes 4055048 | tf_op jit(solution)/shard_map/ppermute | solution.py:68
  47.0 8.6 %collective-permute-start.4 = (bf16[640,256]{1,0:T(8,128)(2,1)S(1)}, bf16[640,256]{1,0:T(8,128)(2,1)}, u32[]{:S(2)}, u32[]{:S(2)}) collective-permute-start(bf16[640,256]{1,0:T(8,128)(2,1)S(1)} %copy-done.6), channel_id=1, source_target_pairs={{0,2},{2,0},{1,3},{3,1},{4,6},{6,4},{5,7},{7,5},{8,10},{10,8},{9,1... | collective-permute-start | bytes 983048 | tf_op jit(solution)/shard_map/ppermute | solution.py:68
  60.2 24.6 %all-to-all-start.1 = ((bf16[4,144,1280]{2,1,0:T(8,128)(2,1)}), bf16[4,144,1280]{2,1,0:T(8,128)(2,1)S(1)}, u32[]{:S(2)}, u32[]{:S(2)}) async-start(bf16[4,144,1280]{2,1,0:T(8,128)(2,1)} %pad_maximum_fusion.2), calls=%async_computation.1 | async-start | bytes 2949120 | tf_op jit(solution)/shard_map/all_to_all | solution.py:409
  88.8 29.6 %collective-permute-start.17 = (bf16[1280,256]{1,0:T(8,128)(2,1)}, bf16[1280,256]{1,0:T(8,128)(2,1)}, u32[]{:S(2)}, u32[]{:S(2)}) collective-permute-start(bf16[1280,256]{1,0:T(8,128)(2,1)} %pad_maximum_fusion.8), channel_id=1, source_target_pairs={{0,8},{4,12},{1,9},{5,13},{2,10},{6,14},{3,11},{7,15},{16,24},{20,... | collective-permute-start | bytes 1966088 | tf_op jit(solution)/shard_map/ppermute | solution.py:435
  90.0 33.1 %collective-permute-start.16 = (bf16[1280,256]{1,0:T(8,128)(2,1)}, bf16[1280,256]{1,0:T(8,128)(2,1)}, u32[]{:S(2)}, u32[]{:S(2)}) collective-permute-start(bf16[1280,256]{1,0:T(8,128)(2,1)} %pad_maximum_fusion.8), channel_id=1, source_target_pairs={{0,4},{4,8},{8,12},{1,5},{5,9},{9,13},{2,6},{6,10},{10,14},{3,7},{... | collective-permute-start | bytes 1966088 | tf_op jit(solution)/shard_map/ppermute | solution.py:434
  104.4 10.3 %collective-permute-start.19 = (bf16[2,16,5120]{2,1,0:T(8,128)(2,1)S(1)}, bf16[2,16,5120]{2,1,0:T(8,128)(2,1)S(1)}, u32[]{:S(2)}, u32[]{:S(2)}) collective-permute-start(bf16[2,16,5120]{2,1,0:T(8,128)(2,1)S(1)} %pad_maximum_fusion.13), channel_id=1, source_target_pairs={{0,16},{16,32},{32,48},{48,0},{1,17},{17,33},{33,49},{49,1},{2,18}... | collective-permute-start | bytes 983048 | tf_op jit(solution)/shard_map/ppermute | solution.py:72
  108.1 9.9 %collective-permute-start.20 = (bf16[2,16,5120]{2,1,0:T(8,128)(2,1)S(1)}, bf16[2,16,5120]{2,1,0:T(8,128)(2,1)S(1)}, u32[]{:S(2)}, u32[]{:S(2)}) collective-permute-start(bf16[2,16,5120]{2,1,0:T(8,128)(2,1)S(1)} %pad_maximum_fusion.13), channel_id=1, source_target_pairs={{0,48},{16,0},{32,16},{48,32},{1,49},{17,1},{33,17},{49,33},{2,50}... | collective-permute-start | bytes 983048 | tf_op jit(solution)/shard_map/ppermute | solution.py:72
  110.2 14.5 %collective-permute-start.9 = (bf16[16,5120]{1,0:T(8,128)(2,1)S(1)}, bf16[16,5120]{1,0:T(8,128)(2,1)S(1)}, u32[]{:S(2)}, u32[]{:S(2)}) collective-permute-start(bf16[16,5120]{1,0:T(8,128)(2,1)S(1)} %slice_bitcast_fusion.7), channel_id=1, source_target_pairs={{0,16},{16,32},{32,48},{48,0},{1,17},{17,33},{33,49},{49,1},{2,18}... | collective-permute-start | bytes 491528 | tf_op jit(solution)/shard_map/ppermute | solution.py:72
  114.7 10.7 %collective-permute-start.10 = (bf16[16,5120]{1,0:T(8,128)(2,1)S(1)}, bf16[16,5120]{1,0:T(8,128)(2,1)S(1)}, u32[]{:S(2)}, u32[]{:S(2)}) collective-permute-start(bf16[16,5120]{1,0:T(8,128)(2,1)S(1)} %slice_bitcast_fusion.6), channel_id=1, source_target_pairs={{0,48},{16,0},{32,16},{48,32},{1,49},{17,1},{33,17},{49,33},{2,50}... | collective-permute-start | bytes 491528 | tf_op jit(solution)/shard_map/ppermute | solution.py:72
  118.3 13.9 %collective-permute-start.22 = (bf16[16,5120]{1,0:T(8,128)(2,1)S(1)}, bf16[16,5120]{1,0:T(8,128)(2,1)S(1)}, u32[]{:S(2)}, u32[]{:S(2)}) collective-permute-start(bf16[16,5120]{1,0:T(8,128)(2,1)S(1)} %slice_bitcast_fusion.4), channel_id=1, source_target_pairs={{0,48},{16,0},{32,16},{48,32},{1,49},{17,1},{33,17},{49,33},{2,50}... | collective-permute-start | bytes 491528 | tf_op jit(solution)/shard_map/ppermute | solution.py:72
  135.1 9.0 %collective-permute-start.23 = (bf16[128,1024]{1,0:T(8,128)(2,1)S(1)}, bf16[128,1024]{1,0:T(8,128)(2,1)S(1)}, u32[]{:S(2)}, u32[]{:S(2)}) collective-permute-start(bf16[128,1024]{1,0:T(8,128)(2,1)S(1)} %constant_dynamic-update-slice_fusion.25), channel_id=1, source_target_pairs={{0,64},{64,0},{1,65},{65,1},{2,66},{66,2},{3,67},{67,3},{4,68},{68... | collective-permute-start | bytes 786440 | tf_op jit(solution)/shard_map/ppermute | solution.py:68
  141.0 9.2 %collective-permute-start.12 = (bf16[2,128,1024]{2,1,0:T(8,128)(2,1)S(1)}, bf16[2,128,1024]{2,1,0:T(8,128)(2,1)S(1)}, u32[]{:S(2)}, u32[]{:S(2)}) collective-permute-start(bf16[2,128,1024]{2,1,0:T(8,128)(2,1)S(1)} %pad_maximum_fusion.9), channel_id=1, source_target_pairs={{0,16},{16,32},{32,48},{48,0},{1,17},{17,33},{33,49},{49,1},{2,18}... | collective-permute-start | bytes 1572872 | tf_op jit(solution)/shard_map/ppermute | solution.py:72
  144.1 9.3 %collective-permute-start.13 = (bf16[2,128,1024]{2,1,0:T(8,128)(2,1)S(1)}, bf16[2,128,1024]{2,1,0:T(8,128)(2,1)S(1)}, u32[]{:S(2)}, u32[]{:S(2)}) collective-permute-start(bf16[2,128,1024]{2,1,0:T(8,128)(2,1)S(1)} %pad_maximum_fusion.9), channel_id=1, source_target_pairs={{0,48},{16,0},{32,16},{48,32},{1,49},{17,1},{33,17},{49,33},{2,50}... | collective-permute-start | bytes 1572872 | tf_op jit(solution)/shard_map/ppermute | solution.py:72
  144.2 15.6 %collective-permute-start.24 = (bf16[2,128,1024]{2,1,0:T(8,128)(2,1)S(1)}, bf16[2,128,1024]{2,1,0:T(8,128)(2,1)S(1)}, u32[]{:S(2)}, u32[]{:S(2)}) collective-permute-start(bf16[2,128,1024]{2,1,0:T(8,128)(2,1)S(1)} %pad_maximum_fusion.10), channel_id=1, source_target_pairs={{0,16},{16,32},{32,48},{48,0},{1,17},{17,33},{33,49},{49,1},{2,18}... | collective-permute-start | bytes 1572872 | tf_op jit(solution)/shard_map/ppermute | solution.py:72
  146.9 16.4 %collective-permute-start.25 = (bf16[2,128,1024]{2,1,0:T(8,128)(2,1)S(1)}, bf16[2,128,1024]{2,1,0:T(8,128)(2,1)S(1)}, u32[]{:S(2)}, u32[]{:S(2)}) collective-permute-start(bf16[2,128,1024]{2,1,0:T(8,128)(2,1)S(1)} %pad_maximum_fusion.10), channel_id=1, source_target_pairs={{0,48},{16,0},{32,16},{48,32},{1,49},{17,1},{33,17},{49,33},{2,50}... | collective-permute-start | bytes 1572872 | tf_op jit(solution)/shard_map/ppermute | solution.py:72
  150.2 15.1 %collective-permute-start.14 = (bf16[128,1024]{1,0:T(8,128)(2,1)S(1)}, bf16[128,1024]{1,0:T(8,128)(2,1)S(1)}, u32[]{:S(2)}, u32[]{:S(2)}) collective-permute-start(bf16[128,1024]{1,0:T(8,128)(2,1)S(1)} %slice_bitcast_fusion.3), channel_id=1, source_target_pairs={{0,16},{16,32},{32,48},{48,0},{1,17},{17,33},{33,49},{49,1},{2,18}... | collective-permute-start | bytes 786440 | tf_op jit(solution)/shard_map/ppermute | solution.py:72
  153.5 15.0 %collective-permute-start.15 = (bf16[128,1024]{1,0:T(8,128)(2,1)S(1)}, bf16[128,1024]{1,0:T(8,128)(2,1)S(1)}, u32[]{:S(2)}, u32[]{:S(2)}) collective-permute-start(bf16[128,1024]{1,0:T(8,128)(2,1)S(1)} %slice_bitcast_fusion.2), channel_id=1, source_target_pairs={{0,48},{16,0},{32,16},{48,32},{1,49},{17,1},{33,17},{49,33},{2,50}... | collective-permute-start | bytes 786440 | tf_op jit(solution)/shard_map/ppermute | solution.py:72
  159.8 11.2 %collective-permute-start.26 = (bf16[128,1024]{1,0:T(8,128)(2,1)S(1)}, bf16[128,1024]{1,0:T(8,128)(2,1)S(1)}, u32[]{:S(2)}, u32[]{:S(2)}) collective-permute-start(bf16[128,1024]{1,0:T(8,128)(2,1)S(1)} %slice_bitcast_fusion.1), channel_id=1, source_target_pairs={{0,16},{16,32},{32,48},{48,0},{1,17},{17,33},{33,49},{49,1},{2,18}... | collective-permute-start | bytes 786440 | tf_op jit(solution)/shard_map/ppermute | solution.py:72
  163.3 10.8 %collective-permute-start.27 = (bf16[128,1024]{1,0:T(8,128)(2,1)S(1)}, bf16[128,1024]{1,0:T(8,128)(2,1)S(1)}, u32[]{:S(2)}, u32[]{:S(2)}) collective-permute-start(bf16[128,1024]{1,0:T(8,128)(2,1)S(1)} %slice_bitcast_fusion), channel_id=1, source_target_pairs={{0,48},{16,0},{32,16},{48,32},{1,49},{17,1},{33,17},{49,33},{2,50}... | collective-permute-start | bytes 786440 | tf_op jit(solution)/shard_map/ppermute | solution.py:72
  183.4 47.5 %all-to-all-start.2 = ((bf16[16,160,512]{2,1,0:T(8,128)(2,1)}), bf16[16,160,512]{2,1,0:T(8,128)(2,1)}, u32[]{:S(2)}, u32[]{:S(2)}) async-start(bf16[16,160,512]{2,1,0:T(8,128)(2,1)} %pad_maximum_fusion), calls=%async_computation.2 | async-start | bytes 5242880 | tf_op jit(solution)/shard_map/all_to_all | solution.py:497
  (34 other events, 377.4 us)
where the time goes:
time: 265 us
  waiting for transfers between devices  86.3 us (33%)
  starting transfers between devices  68.8 us (26%)
  Pallas kernels  40.7 us (15%)
  other arithmetic  21.2 us (8%)
  local copies, waits for them, and re-layouts  17 us (6%)
  between operations  16.2 us (6%)
  matrix products  14.7 us (6%)
    pallas_call x1, Pallas kernels, attention(): pl.pallas_call(attention_kernel, out_shape=jax.ShapeDtypeStruct(text_quer...  33.8 us
    ppermute x16, waiting for transfers between devices, turn(): return lax.ppermute(rows, axis, [(i, (i + by) % 4) for i in range(4)])  28.8 us
    all_to_all x1, waiting for transfers between devices, body(): lax.all_to_all(jnp.concatenate([jnp.broadcast_to(image_kv[None], (CTX_COU...  26.1 us
    ppermute x16, starting transfers between devices, turn(): return lax.ppermute(rows, axis, [(i, (i + by) % 4) for i in range(4)])  20.9 us
    all_to_all x1, starting transfers between devices, body(): lax.all_to_all(jnp.concatenate([jnp.broadcast_to(image_kv[None], (CTX_COU...  16.8 us
    ppermute x8, starting transfers between devices, swap(): return lax.ppermute(rows, axis, [(0, 1), (1, 0)])  11.6 us
    ppermute x8, waiting for transfers between devices, swap(): return lax.ppermute(rows, axis, [(0, 1), (1, 0)])  11 us
    all_to_all x1, waiting for transfers between devices, body(): units = lax.all_to_all(block, DP + ('yl',), split_axis=0, concat_axis=0)  8.85 us
  transfers between devices with their start and end apart: 32, of which 18 were waited for; matrix products, arithmetic and copies ran while one was open for 11% of the time, Pallas kernels for 0%

commit v1 on v0

--- a/solution.py
+++ b/solution.py
@@ -18,7 +18,7 @@
 QUERY_BLOCK = 640
 GROUP = 4
 IMAGES = 512
-PLACE_UNROLL = 4
+PLACE_UNROLL = 8
 CAPACITY = 32
 CHUNK = 16
 UNITS = 24
@@ -140,7 +140,7 @@
         value_wide[rows, :] = text_held[rows, HEAD_DIM:].astype(jnp.float32)
         return unused
 
-    lax.fori_loop(0, WINDOW // 320, widen_text, 0)
+    lax.fori_loop(info[2] // SEQ * 2, (query_offset // SEQ + 1) * 2, widen_text, 0)
     row_in = lax.broadcasted_iota(jnp.int32, (MOST, HEAD_DIM), 0)
 
     def place(step, unused):

time: 265 us -> 258 us (0.974)
  the two profiles are of different devices: /device:TPU:79 before, /device:TPU:111 now
where the time goes in v1:
time: 258 us; the launch traced here: 257 us
  waiting for transfers between devices  83.5 us (32%)
  starting transfers between devices  70.2 us (27%)
  Pallas kernels  34.4 us (13%)
  other arithmetic  21.2 us (8%)
  local copies, waits for them, and re-layouts  17 us (7%)
  between operations  16.2 us (6%)
  matrix products  14.7 us (6%)
    ppermute x16, waiting for transfers between devices, turn(): return lax.ppermute(rows, axis, [(i, (i + by) % 4) for i in range(4)])  28.3 us
    pallas_call x1, Pallas kernels, attention(): pl.pallas_call(attention_kernel, out_shape=jax.ShapeDtypeStruct(text_quer...  27.4 us
    all_to_all x1, waiting for transfers between devices, body(): lax.all_to_all(jnp.concatenate([jnp.broadcast_to(image_kv[None], (CTX_COU...  25.2 us
    all_to_all x1, starting transfers between devices, body(): lax.all_to_all(jnp.concatenate([jnp.broadcast_to(image_kv[None], (CTX_COU...  25.1 us
    ppermute x16, starting transfers between devices, turn(): return lax.ppermute(rows, axis, [(i, (i + by) % 4) for i in range(4)])  17.3 us
    ppermute x8, waiting for transfers between devices, swap(): return lax.ppermute(rows, axis, [(0, 1), (1, 0)])  11.8 us
    ppermute x8, starting transfers between devices, swap(): return lax.ppermute(rows, axis, [(0, 1), (1, 0)])  10.2 us
    ppermute x3, waiting for transfers between devices, body(): lax.ppermute(normed, 'z', [(i, (i + step) % 4) for i in range(4)])  9.59 us
  transfers between devices with their start and end apart: 32, of which 20 were waited for; matrix products, arithmetic and copies ran while one was open for 11% of the time, Pallas kernels for 0%

profile of v1, /device:TPU:111, one launch (start us, length us, event | category | flops | bytes accessed | tf_op | source)
XLA Modules:
  0.0 257.2 jit_solution(5299461810972839703)
XLA Ops:
  7.3 6.8 %all-to-all-start = ((bf16[16,48,1280]{2,1,0:T(8,128)(2,1)}), bf16[16,48,1280]{2,1,0:T(8,128)(2,1)S(1)}, u32[]{:S(2)}, u32[]{:S(2)}) async-start(bf16[16,48,1280]{2,1,0:T(8,128)(2,1)} %broadcast_in_dim.71), calls=%async_computation | async-start | bytes 3932160 | tf_op jit(solution)/shard_map/all_to_all | solution.py:369
  15.5 8.1 %collective-permute-done.2 = bf16[128,1280]{1,0:T(8,128)(2,1)} collective-permute-done((bf16[128,1280]{1,0:T(8,128)(2,1)S(1)}, bf16[128,1280]{1,0:T(8,128)(2,1)}, u32[]{:S(2)}, u32[]{:S(2)}) %collective-permute-start.2) | collective-permute-done | bytes 327712 | tf_op jit(solution)/shard_map/ppermute | solution.py:377
  30.4 8.6 %all-to-all-done = bf16[16,48,1280]{2,1,0:T(8,128)(2,1)S(1)} async-done(((bf16[16,48,1280]{2,1,0:T(8,128)(2,1)}), bf16[16,48,1280]{2,1,0:T(8,128)(2,1)S(1)}, u32[]{:S(2)}, u32[]{:S(2)}) %all-to-all-start) | async-done | bytes 1966112 | tf_op jit(solution)/shard_map/all_to_all | solution.py:369
  40.2 3.7 %multiply_convert_fusion = bf16[1024,384]{1,0:T(8,128)(2,1)S(1)} fusion(bf16[1024,1280]{1,0:T(8,128)(2,1)} %constant_dynamic-update-slice_fusion, bf16[384,1280]{1,0:T(8,128)(2,1)} %bitcast.195), kind=kOutput, calls=%fused_computation.8 | convolution fusion | flops 1008992256 | bytes 4390912 | tf_op jit(solution)/shard_map/dot_general | solution.py:388
  47.9 7.1 %collective-permute-done.4 = bf16[640,256]{1,0:T(8,128)(2,1)} collective-permute-done((bf16[640,256]{1,0:T(8,128)(2,1)S(1)}, bf16[640,256]{1,0:T(8,128)(2,1)}, u32[]{:S(2)}, u32[]{:S(2)}) %collective-permute-start.4) | collective-permute-done | bytes 327712 | tf_op jit(solution)/shard_map/ppermute | solution.py:68
  55.1 2.3 add_convert_fusion
  59.6 6.3 %all-to-all-start.1 = ((bf16[4,144,1280]{2,1,0:T(8,128)(2,1)}), bf16[4,144,1280]{2,1,0:T(8,128)(2,1)S(1)}, u32[]{:S(2)}, u32[]{:S(2)}) async-start(bf16[4,144,1280]{2,1,0:T(8,128)(2,1)} %pad_maximum_fusion.2), calls=%async_computation.1 | async-start | bytes 2949120 | tf_op jit(solution)/shard_map/all_to_all | solution.py:409
  92.2 2.2 collective-permute-start.18
  97.8 3.1 %collective-permute-start.7 = (bf16[2,16,5120]{2,1,0:T(8,128)(2,1)S(1)}, bf16[2,16,5120]{2,1,0:T(8,128)(2,1)S(1)}, u32[]{:S(2)}, u32[]{:S(2)}) collective-permute-start(bf16[2,16,5120]{2,1,0:T(8,128)(2,1)S(1)} %pad_maximum_fusion.12), channel_id=1, source_target_pairs={{0,16},{16,32},{32,48},{48,0},{1,17},{17,33},{33,49},{49,1},{2,18}... | collective-permute-start | bytes 983048 | tf_op jit(solution)/shard_map/ppermute | solution.py:72
  102.5 2.7 %collective-permute-start.19 = (bf16[2,16,5120]{2,1,0:T(8,128)(2,1)S(1)}, bf16[2,16,5120]{2,1,0:T(8,128)(2,1)S(1)}, u32[]{:S(2)}, u32[]{:S(2)}) collective-permute-start(bf16[2,16,5120]{2,1,0:T(8,128)(2,1)S(1)} %pad_maximum_fusion.13), channel_id=1, source_target_pairs={{0,16},{16,32},{32,48},{48,0},{1,17},{17,33},{33,49},{49,1},{2,18}... | collective-permute-start | bytes 983048 | tf_op jit(solution)/shard_map/ppermute | solution.py:72
  109.1 3.7 %collective-permute-done.19 = bf16[2,16,5120]{2,1,0:T(8,128)(2,1)S(1)} collective-permute-done((bf16[2,16,5120]{2,1,0:T(8,128)(2,1)S(1)}, bf16[2,16,5120]{2,1,0:T(8,128)(2,1)S(1)}, u32[]{:S(2)}, u32[]{:S(2)}) %collective-permute-start.19) | collective-permute-done | bytes 327712 | tf_op jit(solution)/shard_map/ppermute | solution.py:72
  112.8 3.2 %collective-permute-done.20 = bf16[2,16,5120]{2,1,0:T(8,128)(2,1)S(1)} collective-permute-done((bf16[2,16,5120]{2,1,0:T(8,128)(2,1)S(1)}, bf16[2,16,5120]{2,1,0:T(8,128)(2,1)S(1)}, u32[]{:S(2)}, u32[]{:S(2)}) %collective-permute-start.20) | collective-permute-done | bytes 327712 | tf_op jit(solution)/shard_map/ppermute | solution.py:72
  122.0 6.0 %convolution_convert_fusion.3 = bf16[128,1024]{1,0:T(8,128)(2,1)S(1)} fusion(bf16[128,5120]{1,0:T(8,128)(2,1)} %bitcast.169, bf16[5120,1024]{1,0:T(8,128)(2,1)} %param.24), kind=kOutput, calls=%fused_computation.16 | convolution fusion | flops 1342308352 | bytes 12058624 | tf_op jit(solution)/shard_map/dot_general | solution.py:451
  133.2 3.6 %collective-permute-done.11 = bf16[128,1024]{1,0:T(8,128)(2,1)S(1)} collective-permute-done((bf16[128,1024]{1,0:T(8,128)(2,1)S(1)}, bf16[128,1024]{1,0:T(8,128)(2,1)S(1)}, u32[]{:S(2)}, u32[]{:S(2)}) %collective-permute-start.11) | collective-permute-done | bytes 262176 | tf_op jit(solution)/shard_map/ppermute | solution.py:68
  141.6 3.6 %collective-permute-done.12 = bf16[2,128,1024]{2,1,0:T(8,128)(2,1)S(1)} collective-permute-done((bf16[2,128,1024]{2,1,0:T(8,128)(2,1)S(1)}, bf16[2,128,1024]{2,1,0:T(8,128)(2,1)S(1)}, u32[]{:S(2)}, u32[]{:S(2)}) %collective-permute-start.12) | collective-permute-done | bytes 524320 | tf_op jit(solution)/shard_map/ppermute | solution.py:72
  145.3 3.0 %collective-permute-start.14 = (bf16[128,1024]{1,0:T(8,128)(2,1)S(1)}, bf16[128,1024]{1,0:T(8,128)(2,1)S(1)}, u32[]{:S(2)}, u32[]{:S(2)}) collective-permute-start(bf16[128,1024]{1,0:T(8,128)(2,1)S(1)} %slice_bitcast_fusion.3), channel_id=1, source_target_pairs={{0,16},{16,32},{32,48},{48,0},{1,17},{17,33},{33,49},{49,1},{2,18}... | collective-permute-start | bytes 786440 | tf_op jit(solution)/shard_map/ppermute | solution.py:72
  148.4 3.9 %collective-permute-done.24 = bf16[2,128,1024]{2,1,0:T(8,128)(2,1)S(1)} collective-permute-done((bf16[2,128,1024]{2,1,0:T(8,128)(2,1)S(1)}, bf16[2,128,1024]{2,1,0:T(8,128)(2,1)S(1)}, u32[]{:S(2)}, u32[]{:S(2)}) %collective-permute-start.24) | collective-permute-done | bytes 524320 | tf_op jit(solution)/shard_map/ppermute | solution.py:72
  152.3 2.3 collective-permute-start.26
  154.9 3.0 %collective-permute-done.14 = bf16[128,1024]{1,0:T(8,128)(2,1)S(1)} collective-permute-done((bf16[128,1024]{1,0:T(8,128)(2,1)S(1)}, bf16[128,1024]{1,0:T(8,128)(2,1)S(1)}, u32[]{:S(2)}, u32[]{:S(2)}) %collective-permute-start.14) | collective-permute-done | bytes 262176 | tf_op jit(solution)/shard_map/ppermute | solution.py:72
  159.8 3.6 %collective-permute-done.26 = bf16[128,1024]{1,0:T(8,128)(2,1)S(1)} collective-permute-done((bf16[128,1024]{1,0:T(8,128)(2,1)S(1)}, bf16[128,1024]{1,0:T(8,128)(2,1)S(1)}, u32[]{:S(2)}, u32[]{:S(2)}) %collective-permute-start.26) | collective-permute-done | bytes 262176 | tf_op jit(solution)/shard_map/ppermute | solution.py:72
  165.5 6.9 %shard_map.163 = (bf16[256,512]{1,0:T(8,128)(2,1)S(1)}, bf16[128,512]{1,0:T(8,128)(2,1)S(1)}) custom-call(s32[8]{0:T(128)S(1)} %fusion.49.order_ref, bf16[8,128,1024]{2,1,0:T(8,128)(2,1)S(1)} %bitcast_dynamic-update-slice_fusion.2.first_ref, bf16[8,128,1024]{2,1,0:T(8,128)(2,1)S(1)} %bitcast_dynamic-update-slice_fusion.second_ref, ...), custom_call_target="tpu_custom_call" | custom-call | flops 3221225472 | bytes 16777216 | tf_op jit(solution)/shard_map/pallas_call | solution.py:292
  174.7 25.1 %all-to-all-start.2 = ((bf16[16,160,512]{2,1,0:T(8,128)(2,1)}), bf16[16,160,512]{2,1,0:T(8,128)(2,1)}, u32[]{:S(2)}, u32[]{:S(2)}) async-start(bf16[16,160,512]{2,1,0:T(8,128)(2,1)} %pad_maximum_fusion), calls=%async_computation.2 | async-start | bytes 5242880 | tf_op jit(solution)/shard_map/all_to_all | solution.py:497
  204.4 25.2 %all-to-all-done.2.last_ref = bf16[16,160,512]{2,1,0:T(8,128)(2,1)} async-done(((bf16[16,160,512]{2,1,0:T(8,128)(2,1)}), bf16[16,160,512]{2,1,0:T(8,128)(2,1)}, u32[]{:S(2)}, u32[]{:S(2)}) %all-to-all-start.2) | async-done | bytes 2621472 | tf_op jit(solution)/shard_map/all_to_all | solution.py:497
  229.6 27.4 %shard_map.164 = bf16[640,512]{1,0:T(8,128)(2,1)} custom-call(s32[4]{0:T(128)S(1)} %pad_add_fusion.1.info, s32[512]{0:T(512)S(1)} %add.310.image_src, s32[512]{0:T(512)S(1)} %get-tuple-element.67.image_dst, s32[512]{0:T(512)S(1)} %get-tuple-element.66.image_len, s32[9]{0:T(128)S(1)} %fusion.56.blocks_at, bf16[640,512]{1,0:T(8,128)(2,1)S(1)} %copy-done.2, ...), custom_call_target="tpu_custom_call" | custom-call | flops 8000000000 | bytes 8000000 | tf_op jit(solution)/shard_map/pallas_call | solution.py:229
  (246 shorter events, 69.6 us)
Async XLA Ops:
  5.4 8.7 %collective-permute-start = (bf16[128,1280]{1,0:T(8,128)(2,1)S(1)}, bf16[128,1280]{1,0:T(8,128)(2,1)S(1)}, u32[]{:S(2)}, u32[]{:S(2)}) collective-permute-start(bf16[128,1280]{1,0:T(8,128)(2,1)S(1)} %get-tuple-element.36), channel_id=1, source_target_pairs={{0,4},{4,8},{8,12},{12,0},{1,5},{5,9},{9,13},{13,1},{2,6},{6,10},{... | collective-permute-start | bytes 983048 | tf_op jit(solution)/shard_map/ppermute | solution.py:377
  5.4 10.1 %collective-permute-start.1 = (bf16[128,1280]{1,0:T(8,128)(2,1)S(1)}, bf16[128,1280]{1,0:T(8,128)(2,1)S(1)}, u32[]{:S(2)}, u32[]{:S(2)}) collective-permute-start(bf16[128,1280]{1,0:T(8,128)(2,1)S(1)} %get-tuple-element.36), channel_id=1, source_target_pairs={{0,8},{4,12},{8,0},{12,4},{1,9},{5,13},{9,1},{13,5},{2,10},{6,14},... | collective-permute-start | bytes 983048 | tf_op jit(solution)/shard_map/ppermute | solution.py:377
  7.3 16.4 %collective-permute-start.2 = (bf16[128,1280]{1,0:T(8,128)(2,1)S(1)}, bf16[128,1280]{1,0:T(8,128)(2,1)}, u32[]{:S(2)}, u32[]{:S(2)}) collective-permute-start(bf16[128,1280]{1,0:T(8,128)(2,1)S(1)} %get-tuple-element.36), channel_id=1, source_target_pairs={{0,12},{4,0},{8,4},{12,8},{1,13},{5,1},{9,5},{13,9},{2,14},{6,2},{... | collective-permute-start | bytes 983048 | tf_op jit(solution)/shard_map/ppermute | solution.py:377
  7.3 31.7 %all-to-all-start = ((bf16[16,48,1280]{2,1,0:T(8,128)(2,1)}), bf16[16,48,1280]{2,1,0:T(8,128)(2,1)S(1)}, u32[]{:S(2)}, u32[]{:S(2)}) async-start(bf16[16,48,1280]{2,1,0:T(8,128)(2,1)} %broadcast_in_dim.71), calls=%async_computation | async-start | bytes 3932160 | tf_op jit(solution)/shard_map/all_to_all | solution.py:369
  44.9 10.2 %collective-permute-start.5 = (bf16[528,1280]{1,0:T(8,128)(2,1)S(1)}, bf16[528,1280]{1,0:T(8,128)(2,1)}, u32[]{:S(2)}, u32[]{:S(2)}) collective-permute-start(bf16[528,1280]{1,0:T(8,128)(2,1)S(1)} %fusion.1), channel_id=1, source_target_pairs={{0,1},{1,0},{2,3},{3,2},{4,5},{5,4},{6,7},{7,6},{8,9},{9,8},{10,11... | collective-permute-start | bytes 4055048 | tf_op jit(solution)/shard_map/ppermute | solution.py:68
  46.4 8.6 %collective-permute-start.4 = (bf16[640,256]{1,0:T(8,128)(2,1)S(1)}, bf16[640,256]{1,0:T(8,128)(2,1)}, u32[]{:S(2)}, u32[]{:S(2)}) collective-permute-start(bf16[640,256]{1,0:T(8,128)(2,1)S(1)} %copy-done.6), channel_id=1, source_target_pairs={{0,2},{2,0},{1,3},{3,1},{4,6},{6,4},{5,7},{7,5},{8,10},{10,8},{9,1... | collective-permute-start | bytes 983048 | tf_op jit(solution)/shard_map/ppermute | solution.py:68
  59.6 24.7 %all-to-all-start.1 = ((bf16[4,144,1280]{2,1,0:T(8,128)(2,1)}), bf16[4,144,1280]{2,1,0:T(8,128)(2,1)S(1)}, u32[]{:S(2)}, u32[]{:S(2)}) async-start(bf16[4,144,1280]{2,1,0:T(8,128)(2,1)} %pad_maximum_fusion.2), calls=%async_computation.1 | async-start | bytes 2949120 | tf_op jit(solution)/shard_map/all_to_all | solution.py:409
  88.3 28.1 %collective-permute-start.17 = (bf16[1280,256]{1,0:T(8,128)(2,1)}, bf16[1280,256]{1,0:T(8,128)(2,1)}, u32[]{:S(2)}, u32[]{:S(2)}) collective-permute-start(bf16[1280,256]{1,0:T(8,128)(2,1)} %pad_maximum_fusion.8), channel_id=1, source_target_pairs={{0,8},{4,12},{1,9},{5,13},{2,10},{6,14},{3,11},{7,15},{16,24},{20,... | collective-permute-start | bytes 1966088 | tf_op jit(solution)/shard_map/ppermute | solution.py:435
  89.6 28.1 %collective-permute-start.16 = (bf16[1280,256]{1,0:T(8,128)(2,1)}, bf16[1280,256]{1,0:T(8,128)(2,1)}, u32[]{:S(2)}, u32[]{:S(2)}) collective-permute-start(bf16[1280,256]{1,0:T(8,128)(2,1)} %pad_maximum_fusion.8), channel_id=1, source_target_pairs={{0,4},{4,8},{8,12},{1,5},{5,9},{9,13},{2,6},{6,10},{10,14},{3,7},{... | collective-permute-start | bytes 1966088 | tf_op jit(solution)/shard_map/ppermute | solution.py:434
  92.2 8.6 %collective-permute-start.18 = (bf16[16,5120]{1,0:T(8,128)(2,1)}, bf16[16,5120]{1,0:T(8,128)(2,1)S(1)}, u32[]{:S(2)}, u32[]{:S(2)}) collective-permute-start(bf16[16,5120]{1,0:T(8,128)(2,1)} %get-tuple-element.49), channel_id=1, source_target_pairs={{0,64},{64,0},{1,65},{65,1},{2,66},{66,2},{3,67},{67,3},{4,68},{68... | collective-permute-start | bytes 491528 | tf_op jit(solution)/shard_map/ppermute | solution.py:68
  97.8 8.4 %collective-permute-start.7 = (bf16[2,16,5120]{2,1,0:T(8,128)(2,1)S(1)}, bf16[2,16,5120]{2,1,0:T(8,128)(2,1)S(1)}, u32[]{:S(2)}, u32[]{:S(2)}) collective-permute-start(bf16[2,16,5120]{2,1,0:T(8,128)(2,1)S(1)} %pad_maximum_fusion.12), channel_id=1, source_target_pairs={{0,16},{16,32},{32,48},{48,0},{1,17},{17,33},{33,49},{49,1},{2,18}... | collective-permute-start | bytes 983048 | tf_op jit(solution)/shard_map/ppermute | solution.py:72
  102.5 10.3 %collective-permute-start.19 = (bf16[2,16,5120]{2,1,0:T(8,128)(2,1)S(1)}, bf16[2,16,5120]{2,1,0:T(8,128)(2,1)S(1)}, u32[]{:S(2)}, u32[]{:S(2)}) collective-permute-start(bf16[2,16,5120]{2,1,0:T(8,128)(2,1)S(1)} %pad_maximum_fusion.13), channel_id=1, source_target_pairs={{0,16},{16,32},{32,48},{48,0},{1,17},{17,33},{33,49},{49,1},{2,18}... | collective-permute-start | bytes 983048 | tf_op jit(solution)/shard_map/ppermute | solution.py:72
  106.2 9.8 %collective-permute-start.20 = (bf16[2,16,5120]{2,1,0:T(8,128)(2,1)S(1)}, bf16[2,16,5120]{2,1,0:T(8,128)(2,1)S(1)}, u32[]{:S(2)}, u32[]{:S(2)}) collective-permute-start(bf16[2,16,5120]{2,1,0:T(8,128)(2,1)S(1)} %pad_maximum_fusion.13), channel_id=1, source_target_pairs={{0,48},{16,0},{32,16},{48,32},{1,49},{17,1},{33,17},{49,33},{2,50}... | collective-permute-start | bytes 983048 | tf_op jit(solution)/shard_map/ppermute | solution.py:72
  108.4 10.9 %collective-permute-start.9 = (bf16[16,5120]{1,0:T(8,128)(2,1)S(1)}, bf16[16,5120]{1,0:T(8,128)(2,1)S(1)}, u32[]{:S(2)}, u32[]{:S(2)}) collective-permute-start(bf16[16,5120]{1,0:T(8,128)(2,1)S(1)} %slice_bitcast_fusion.7), channel_id=1, source_target_pairs={{0,16},{16,32},{32,48},{48,0},{1,17},{17,33},{33,49},{49,1},{2,18}... | collective-permute-start | bytes 491528 | tf_op jit(solution)/shard_map/ppermute | solution.py:72
  116.4 11.7 %collective-permute-start.22 = (bf16[16,5120]{1,0:T(8,128)(2,1)S(1)}, bf16[16,5120]{1,0:T(8,128)(2,1)S(1)}, u32[]{:S(2)}, u32[]{:S(2)}) collective-permute-start(bf16[16,5120]{1,0:T(8,128)(2,1)S(1)} %slice_bitcast_fusion.4), channel_id=1, source_target_pairs={{0,48},{16,0},{32,16},{48,32},{1,49},{17,1},{33,17},{49,33},{2,50}... | collective-permute-start | bytes 491528 | tf_op jit(solution)/shard_map/ppermute | solution.py:72
  136.9 8.4 %collective-permute-start.12 = (bf16[2,128,1024]{2,1,0:T(8,128)(2,1)S(1)}, bf16[2,128,1024]{2,1,0:T(8,128)(2,1)S(1)}, u32[]{:S(2)}, u32[]{:S(2)}) collective-permute-start(bf16[2,128,1024]{2,1,0:T(8,128)(2,1)S(1)} %pad_maximum_fusion.9), channel_id=1, source_target_pairs={{0,16},{16,32},{32,48},{48,0},{1,17},{17,33},{33,49},{49,1},{2,18}... | collective-permute-start | bytes 1572872 | tf_op jit(solution)/shard_map/ppermute | solution.py:72
  138.8 9.5 %collective-permute-start.13 = (bf16[2,128,1024]{2,1,0:T(8,128)(2,1)S(1)}, bf16[2,128,1024]{2,1,0:T(8,128)(2,1)S(1)}, u32[]{:S(2)}, u32[]{:S(2)}) collective-permute-start(bf16[2,128,1024]{2,1,0:T(8,128)(2,1)S(1)} %pad_maximum_fusion.9), channel_id=1, source_target_pairs={{0,48},{16,0},{32,16},{48,32},{1,49},{17,1},{33,17},{49,33},{2,50}... | collective-permute-start | bytes 1572872 | tf_op jit(solution)/shard_map/ppermute | solution.py:72
  139.7 12.6 %collective-permute-start.24 = (bf16[2,128,1024]{2,1,0:T(8,128)(2,1)S(1)}, bf16[2,128,1024]{2,1,0:T(8,128)(2,1)S(1)}, u32[]{:S(2)}, u32[]{:S(2)}) collective-permute-start(bf16[2,128,1024]{2,1,0:T(8,128)(2,1)S(1)} %pad_maximum_fusion.10), channel_id=1, source_target_pairs={{0,16},{16,32},{32,48},{48,0},{1,17},{17,33},{33,49},{49,1},{2,18}... | collective-permute-start | bytes 1572872 | tf_op jit(solution)/shard_map/ppermute | solution.py:72
  141.6 13.0 %collective-permute-start.25 = (bf16[2,128,1024]{2,1,0:T(8,128)(2,1)S(1)}, bf16[2,128,1024]{2,1,0:T(8,128)(2,1)S(1)}, u32[]{:S(2)}, u32[]{:S(2)}) collective-permute-start(bf16[2,128,1024]{2,1,0:T(8,128)(2,1)S(1)} %pad_maximum_fusion.10), channel_id=1, source_target_pairs={{0,48},{16,0},{32,16},{48,32},{1,49},{17,1},{33,17},{49,33},{2,50}... | collective-permute-start | bytes 1572872 | tf_op jit(solution)/shard_map/ppermute | solution.py:72
  145.3 12.6 %collective-permute-start.14 = (bf16[128,1024]{1,0:T(8,128)(2,1)S(1)}, bf16[128,1024]{1,0:T(8,128)(2,1)S(1)}, u32[]{:S(2)}, u32[]{:S(2)}) collective-permute-start(bf16[128,1024]{1,0:T(8,128)(2,1)S(1)} %slice_bitcast_fusion.3), channel_id=1, source_target_pairs={{0,16},{16,32},{32,48},{48,0},{1,17},{17,33},{33,49},{49,1},{2,18}... | collective-permute-start | bytes 786440 | tf_op jit(solution)/shard_map/ppermute | solution.py:72
  148.3 11.5 %collective-permute-start.15 = (bf16[128,1024]{1,0:T(8,128)(2,1)S(1)}, bf16[128,1024]{1,0:T(8,128)(2,1)S(1)}, u32[]{:S(2)}, u32[]{:S(2)}) collective-permute-start(bf16[128,1024]{1,0:T(8,128)(2,1)S(1)} %slice_bitcast_fusion.2), channel_id=1, source_target_pairs={{0,48},{16,0},{32,16},{48,32},{1,49},{17,1},{33,17},{49,33},{2,50}... | collective-permute-start | bytes 786440 | tf_op jit(solution)/shard_map/ppermute | solution.py:72
  152.3 11.2 %collective-permute-start.26 = (bf16[128,1024]{1,0:T(8,128)(2,1)S(1)}, bf16[128,1024]{1,0:T(8,128)(2,1)S(1)}, u32[]{:S(2)}, u32[]{:S(2)}) collective-permute-start(bf16[128,1024]{1,0:T(8,128)(2,1)S(1)} %slice_bitcast_fusion.1), channel_id=1, source_target_pairs={{0,16},{16,32},{32,48},{48,0},{1,17},{17,33},{33,49},{49,1},{2,18}... | collective-permute-start | bytes 786440 | tf_op jit(solution)/shard_map/ppermute | solution.py:72
  154.6 10.8 %collective-permute-start.27 = (bf16[128,1024]{1,0:T(8,128)(2,1)S(1)}, bf16[128,1024]{1,0:T(8,128)(2,1)S(1)}, u32[]{:S(2)}, u32[]{:S(2)}) collective-permute-start(bf16[128,1024]{1,0:T(8,128)(2,1)S(1)} %slice_bitcast_fusion), channel_id=1, source_target_pairs={{0,48},{16,0},{32,16},{48,32},{1,49},{17,1},{33,17},{49,33},{2,50}... | collective-permute-start | bytes 786440 | tf_op jit(solution)/shard_map/ppermute | solution.py:72
  174.7 54.9 %all-to-all-start.2 = ((bf16[16,160,512]{2,1,0:T(8,128)(2,1)}), bf16[16,160,512]{2,1,0:T(8,128)(2,1)}, u32[]{:S(2)}, u32[]{:S(2)}) async-start(bf16[16,160,512]{2,1,0:T(8,128)(2,1)} %pad_maximum_fusion), calls=%async_computation.2 | async-start | bytes 5242880 | tf_op jit(solution)/shard_map/all_to_all | solution.py:497
  (34 other events, 391.4 us)
